TPU v7x, 256 devices: a whole 4x4x8 slice. The times are simulated.
256 devices in a mesh: spec: 32 (over x_lo, z, core), bucket: 8 (over y, x_hi).
Axes of the slice: x: 4 (x_hi: 2, x_lo: 2; x = x_hi * 2 + x_lo), y: 4, z: 8, core: 2. Of those that a mesh axis runs over, the one named last changes fastest.
Arguments:
- spectra: bfloat16 [2048, 65536], P('bucket', 'spec'), may hold values from 0 to 20
- theory: bfloat16 [512, 65536], P('bucket', 'spec'), may hold values from 0 to 16
- cand: int32 [2048, 128], P('bucket'), may hold values from 0 to 511
- half: int32 [128], P('spec'), may hold values from 25 to 75
Outputs:
- cand_scores: float32 [2048, 128], P('bucket')
- peptide_score: float32 [512], P(('spec', 'bucket'))
All inputs are finite; a program needn't handle non-finite values.
Results may differ from a plain program's by a relative error of at most 0.0041.
Values may be sent and summed in bfloat16 or wider, within the bound.
No kernel may reach another device: no remote copies, remote signals or barrier semaphores. Data moves between devices by JAX's collectives and lax.ppermute only.
A program may use at most 64 MiB of HBM per device.

v0:
```python
import jax
import jax.numpy as jnp
from jax import lax
from jax.sharding import PartitionSpec as P

HALF = 75
REGION = 512


def extended_2(block, sides, width):
    for axis, dim in sides:
        count = lax.axis_size(axis)
        forward = [(i, i + 1) for i in range(count - 1)]
        backward = [(target, source) for source, target in forward]
        low = lax.ppermute(
            lax.slice_in_dim(block, block.shape[dim] - width, None, axis=dim), axis, forward
        )
        high = lax.ppermute(lax.slice_in_dim(block, 0, width, axis=dim), axis, backward)
        block = jnp.concatenate([low, block, high], axis=dim)
    return block


def broadcast(value, axis, source):
    kept = jnp.where(lax.axis_index(axis) == source, value, 0).astype(value.dtype)
    return lax.psum(kept, axis)


def make_band(widths):
    block_iota = lax.broadcasted_iota(jnp.int32, (3, 128, 128), 0)
    input_iota = lax.broadcasted_iota(jnp.int32, (3, 128, 128), 1)
    output_iota = lax.broadcasted_iota(jnp.int32, (3, 128, 128), 2)
    offset = 128 * (block_iota - 1) + input_iota - output_iota
    return jnp.abs(offset)[None] <= widths[:, None, None, None]


def zscores(score_tile, cand_ids):
    average = jnp.mean(score_tile, axis=1, keepdims=True)
    spread = jnp.mean(jnp.square(score_tile - average), axis=1, keepdims=True)
    picked = jnp.take_along_axis(score_tile, cand_ids, axis=1)
    return (picked - average) * lax.rsqrt(spread + 1e-06)


def against(processed, received):
    return lax.dot_general(
        processed, received, (((1,), (1,)), ((), ())), preferred_element_type=jnp.float32
    )


def on_device(spectra, theory, cand, half):
    row_count, bin_count = spectra.shape
    spec_count = lax.axis_size("spec")
    bucket_count = lax.axis_size("bucket")
    per_bucket = theory.shape[0]
    peptides_all = per_bucket * bucket_count
    position = lax.axis_index("spec")
    extended = extended_2(spectra, (("spec", 1),), HALF)
    bin_widths = jnp.repeat(half, REGION)
    tile_count = bin_count // 128
    padded = jnp.pad(extended, ((0, 0), (128 - HALF, 128 - HALF)))
    tile_view = padded.reshape(row_count, tile_count + 2, 128)
    band_weights = make_band(jnp.repeat(half, REGION // 128)).astype(jnp.bfloat16)
    window_sums = jnp.zeros((row_count, tile_count, 128), jnp.float32)
    for k in range(3):
        window_sums = window_sums + jnp.einsum(
            "rtc,tcd->rtd",
            tile_view[:, k : k + tile_count],
            band_weights[:, k],
            preferred_element_type=jnp.float32,
        )
    window_sums = window_sums.reshape(row_count, bin_count)
    divisor = (2 * bin_widths + 1).astype(jnp.float32)
    processed = (spectra.astype(jnp.float32) - window_sums / divisor).astype(jnp.bfloat16)
    zero_tile = jnp.zeros((row_count, peptides_all), jnp.float32)

    def rooted_step(step_index, running):
        received = broadcast(theory, "bucket", step_index)
        return lax.dynamic_update_slice(
            running, against(processed, received), (jnp.int32(0), step_index * per_bucket)
        )

    score_tile = lax.fori_loop(0, bucket_count, rooted_step, zero_tile)
    summed = lax.psum(score_tile, "spec")
    cand_scores = zscores(summed, cand)
    col_share = cand.shape[1] // spec_count
    local_ids = lax.dynamic_slice_in_dim(cand, position * col_share, col_share, 1)
    local_scores = lax.dynamic_slice_in_dim(cand_scores, position * col_share, col_share, 1)
    partial_value = jax.ops.segment_sum(
        jax.nn.softplus(local_scores).reshape(-1), local_ids.reshape(-1), num_segments=peptides_all
    )
    mean_load = cand.shape[1] * row_count / per_bucket
    peptide_score = (
        lax.psum_scatter(partial_value, ("spec", "bucket"), scatter_dimension=0, tiled=True)
        / mean_load
    )
    return (cand_scores, peptide_score)


def solution(mesh):
    return jax.shard_map(
        on_device,
        mesh=mesh,
        in_specs=(P("bucket", "spec"), P("bucket", "spec"), P("bucket", None), P("spec")),
        out_specs=(P("bucket", None), P(("spec", "bucket"))),
        check_vma=False,
    )
```

profile of v0, /device:TPU:1, one launch (start us, length us, event | category | flops | bytes accessed | tf_op | source)
XLA Modules:
  0.0 1349.8 jit_solution(1085945206522732928)
XLA Ops:
  8.0 1.5 copy.14
  9.6 4.9 collective-permute-start
  14.5 1.9 collective-permute-start.1
  16.4 0.1 subtract_abs_fusion
  16.6 0.1 broadcast_in_dim.32
  16.6 0.1 le.27
  16.7 0.1 broadcast_bitcast_fusion
  16.8 0.5 broadcast_compare_fusion
  17.3 0.1 constant_dynamic-slice_fusion
  17.4 0.1 reshape.69
  17.6 2.2 collective-permute-done.1
  19.8 1.4 concatenate.3
  21.3 0.3 pad.4
  21.6 0.4 fusion.2
  22.0 0.4 fusion.4
  22.4 1.8 add_add_fusion
  24.3 1.9 copy.20
  26.2 1.6 subtract_convert_fusion
  27.9 737.3 %while.15 = (s32[]{:T(128)}, f32[256,512]{0,1:T(8,128)S(1)}, bf16[64,2048]{1,0:T(8,128)(2,1)S(1)}, bf16[256,2048]{1,0:T(8,128)(2,1)S(1)}, s32[]{:T(128)}, /*index=5*/s32[]{:T(128)}, s32[]{:T(128)}, s32[]{:T(128)}, u32[]{:T(128)}) while((s32[]{:T(128)}, f32[256,512]{0,1:T(8,128)S(1)}, bf16[64,2048]{1,0:T(8,128)(2,1)S(1)}, ...), condition=%wide.region_2.3_spmd, body=%wide.region_0.2_spmd.sunk | while | flops 67371016 | bytes 3473621 | solution.py:81
  27.9 0.0 all-reduce.7.cloned.1.call-start
  28.0 0.7 broadcast_select_fusion.2
  28.7 89.5 %all-reduce.7.cloned.1.call-done = bf16[64,2048]{1,0:T(8,128)(2,1)} async-done(((bf16[64,2048]{1,0:T(8,128)(2,1)}), bf16[64,2048]{1,0:T(8,128)(2,1)}) %all-reduce.7.cloned.1.call-update) | async-done | bytes 262160 | tf_op jit(solution)/shard_map/while/body/eval_jaxpr/psum | solution.py:25
  118.2 1.4 fusion.19
  119.6 0.0 all-reduce.7.cloned.1.call-start
  119.6 0.7 broadcast_select_fusion.2
  120.4 90.1 %all-reduce.7.cloned.1.call-done = bf16[64,2048]{1,0:T(8,128)(2,1)} async-done(((bf16[64,2048]{1,0:T(8,128)(2,1)}), bf16[64,2048]{1,0:T(8,128)(2,1)}) %all-reduce.7.cloned.1.call-update) | async-done | bytes 262160 | tf_op jit(solution)/shard_map/while/body/eval_jaxpr/psum | solution.py:25
  210.5 1.4 fusion.19
  211.9 0.0 all-reduce.7.cloned.1.call-start
  212.0 0.7 broadcast_select_fusion.2
  212.8 90.1 %all-reduce.7.cloned.1.call-done = bf16[64,2048]{1,0:T(8,128)(2,1)} async-done(((bf16[64,2048]{1,0:T(8,128)(2,1)}), bf16[64,2048]{1,0:T(8,128)(2,1)}) %all-reduce.7.cloned.1.call-update) | async-done | bytes 262160 | tf_op jit(solution)/shard_map/while/body/eval_jaxpr/psum | solution.py:25
  302.9 1.4 fusion.19
  304.3 0.0 all-reduce.7.cloned.1.call-start
  304.4 0.7 broadcast_select_fusion.2
  305.1 89.8 %all-reduce.7.cloned.1.call-done = bf16[64,2048]{1,0:T(8,128)(2,1)} async-done(((bf16[64,2048]{1,0:T(8,128)(2,1)}), bf16[64,2048]{1,0:T(8,128)(2,1)}) %all-reduce.7.cloned.1.call-update) | async-done | bytes 262160 | tf_op jit(solution)/shard_map/while/body/eval_jaxpr/psum | solution.py:25
  394.9 1.4 fusion.19
  396.3 0.0 all-reduce.7.cloned.1.call-start
  396.4 0.7 broadcast_select_fusion.2
  397.2 89.8 %all-reduce.7.cloned.1.call-done = bf16[64,2048]{1,0:T(8,128)(2,1)} async-done(((bf16[64,2048]{1,0:T(8,128)(2,1)}), bf16[64,2048]{1,0:T(8,128)(2,1)}) %all-reduce.7.cloned.1.call-update) | async-done | bytes 262160 | tf_op jit(solution)/shard_map/while/body/eval_jaxpr/psum | solution.py:25
  487.0 1.4 fusion.19
  488.4 0.0 all-reduce.7.cloned.1.call-start
  488.5 0.7 broadcast_select_fusion.2
  489.2 89.8 %all-reduce.7.cloned.1.call-done = bf16[64,2048]{1,0:T(8,128)(2,1)} async-done(((bf16[64,2048]{1,0:T(8,128)(2,1)}), bf16[64,2048]{1,0:T(8,128)(2,1)}) %all-reduce.7.cloned.1.call-update) | async-done | bytes 262160 | tf_op jit(solution)/shard_map/while/body/eval_jaxpr/psum | solution.py:25
  579.0 1.4 fusion.19
  580.4 0.0 all-reduce.7.cloned.1.call-start
  580.5 0.7 broadcast_select_fusion.2
  581.3 90.1 %all-reduce.7.cloned.1.call-done = bf16[64,2048]{1,0:T(8,128)(2,1)} async-done(((bf16[64,2048]{1,0:T(8,128)(2,1)}), bf16[64,2048]{1,0:T(8,128)(2,1)}) %all-reduce.7.cloned.1.call-update) | async-done | bytes 262160 | tf_op jit(solution)/shard_map/while/body/eval_jaxpr/psum | solution.py:25
  671.4 1.4 fusion.19
  672.8 0.0 all-reduce.7.cloned.1.call-start
  672.9 0.7 broadcast_select_fusion.2
  673.6 90.1 %all-reduce.7.cloned.1.call-done = bf16[64,2048]{1,0:T(8,128)(2,1)} async-done(((bf16[64,2048]{1,0:T(8,128)(2,1)}), bf16[64,2048]{1,0:T(8,128)(2,1)}) %all-reduce.7.cloned.1.call-update) | async-done | bytes 262160 | tf_op jit(solution)/shard_map/while/body/eval_jaxpr/psum | solution.py:25
  763.8 1.4 fusion.19
  765.2 0.0 all-reduce.5.cloned.1.call-start
  765.2 0.7 copy-done.2
  766.0 0.0 all-reduce.5.cloned.1.call-update
  766.1 227.0 %all-reduce.5.cloned.1.call-done = f32[256,512]{0,1:T(8,128)} async-done(((f32[256,512]{0,1:T(8,128)}), f32[256,512]{0,1:T(8,128)}) %all-reduce.5.cloned.1.call-update) | async-done | bytes 524304 | tf_op jit(solution)/shard_map/psum | solution.py:82
  993.0 1.2 reduce_sum.18
  994.2 1.1 multiply_reduce_fusion
  995.4 260.6 %gather_fusion = f32[32768]{0:T(1024)S(1)} fusion(f32[256,512]{0,1:T(8,128)S(1)} %copy-done, s32[32768]{0:T(1024)S(1)} %fusion.8), kind=kCustom, calls=%fused_computation | custom fusion | bytes 524288 | tf_op jit(solution)/shard_map/jit(take_along_axis)/gather | solution.py:39
  1256.0 0.1 fusion.7
  1256.1 0.2 compare_select_fusion
  1256.3 0.1 reshape.71
  1256.4 7.6 scatter_custom_fusion
  1264.0 77.8 %all-reduce.1 = f32[512]{0:T(512)S(1)} all-reduce(f32[512]{0:T(512)S(1)} %scatter_custom_fusion), channel_id=2, replica_groups=mesh['spec'=32,'bucket'=8] {'spec','bucket'}, use_global_device_ids=true, to_apply=%region_7.8.clone | all-reduce | flops 512 | bytes 4096
  1341.8 0.6 dynamic-slice_multiply_fusion
  (28 shorter events, 0.3 us)
Async XLA Ops:
  8.0 8.6 copy-start.5
  8.0 9.3 copy-start.3
  9.6 8.0 collective-permute-start
  14.5 5.3 collective-permute-start.1
  26.2 1.7 copy-start.1
  27.9 90.3 %all-reduce.7.cloned.1.call-start = ((), (), s32[]{:S(2)}) async-start(), calls=%async_computation.1 | async-start | bytes 524288 | tf_op jit(solution)/shard_map/while/body/eval_jaxpr/psum | solution.py:25
  119.6 91.0 %all-reduce.7.cloned.1.call-start = ((), (), s32[]{:S(2)}) async-start(), calls=%async_computation.1 | async-start | bytes 524288 | tf_op jit(solution)/shard_map/while/body/eval_jaxpr/psum | solution.py:25
  211.9 91.0 %all-reduce.7.cloned.1.call-start = ((), (), s32[]{:S(2)}) async-start(), calls=%async_computation.1 | async-start | bytes 524288 | tf_op jit(solution)/shard_map/while/body/eval_jaxpr/psum | solution.py:25
  304.3 90.6 %all-reduce.7.cloned.1.call-start = ((), (), s32[]{:S(2)}) async-start(), calls=%async_computation.1 | async-start | bytes 524288 | tf_op jit(solution)/shard_map/while/body/eval_jaxpr/psum | solution.py:25
  396.3 90.6 %all-reduce.7.cloned.1.call-start = ((), (), s32[]{:S(2)}) async-start(), calls=%async_computation.1 | async-start | bytes 524288 | tf_op jit(solution)/shard_map/while/body/eval_jaxpr/psum | solution.py:25
  488.4 90.6 %all-reduce.7.cloned.1.call-start = ((), (), s32[]{:S(2)}) async-start(), calls=%async_computation.1 | async-start | bytes 524288 | tf_op jit(solution)/shard_map/while/body/eval_jaxpr/psum | solution.py:25
  580.4 91.0 %all-reduce.7.cloned.1.call-start = ((), (), s32[]{:S(2)}) async-start(), calls=%async_computation.1 | async-start | bytes 524288 | tf_op jit(solution)/shard_map/while/body/eval_jaxpr/psum | solution.py:25
  672.8 91.0 %all-reduce.7.cloned.1.call-start = ((), (), s32[]{:S(2)}) async-start(), calls=%async_computation.1 | async-start | bytes 524288 | tf_op jit(solution)/shard_map/while/body/eval_jaxpr/psum | solution.py:25
  765.2 0.8 copy-start.2
  765.2 227.9 %all-reduce.5.cloned.1.call-start = ((), (), s32[]{:S(2)}) async-start(), calls=%async_computation | async-start | bytes 1048576 | tf_op jit(solution)/shard_map/psum | solution.py:82
  993.0 2.4 copy-start
  1256.1 86.3 %copy-start.4 = (f32[256,128]{1,0:T(8,128)}, f32[256,128]{1,0:T(8,128)S(1)}, u32[]{:S(2)}) copy-start(f32[256,128]{1,0:T(8,128)S(1)} %fusion.7) | copy-start | bytes 393220
Sparse Core Ops, SparseCore 0:
  31.5 86.5 all-reduce.6
  123.2 87.2 all-reduce.6
  215.6 87.2 all-reduce.6
  307.6 87.2 all-reduce.6
  399.7 87.2 all-reduce.6
  491.7 87.2 all-reduce.6
  584.1 87.2 all-reduce.6
  676.4 87.2 all-reduce.6
Sparse Core Ops, SparseCore 1:
  768.3 224.7 all-reduce.4
where the time goes:
time: 1350 us
  waiting for transfers between devices  949 us (70%)
  local copies, waits for them, and re-layouts  267 us (20%)
  blocking collectives  77.8 us (6%)
  other arithmetic  18.9 us (1%)
  between operations  15.7 us (1%)
  matrix products  13.8 us (1%)
    psum x8, waiting for transfers between devices, broadcast(): return lax.psum(kept, axis)  720 us
    gather x1, local copies, waits for them, and re-layouts, zscores(): picked = jnp.take_along_axis(score_tile, cand_ids, axis=1)  261 us
    psum x1, waiting for transfers between devices, on_device(): summed = lax.psum(score_tile, 'spec')  227 us
    unnamed x1, blocking collectives  77.8 us
  transfers between devices with their start and end apart: 11, of which 10 were waited for; matrix products, arithmetic and copies ran while one was open for 0% of the time, Pallas kernels for 0%

commit v1 on v0

--- a/solution.py
+++ b/solution.py
@@ -79,7 +79,7 @@
         )
 
     score_tile = lax.fori_loop(0, bucket_count, rooted_step, zero_tile)
-    summed = lax.psum(score_tile, "spec")
+    summed = jnp.sum(lax.all_gather(score_tile, "spec"), axis=0)
     cand_scores = zscores(summed, cand)
     col_share = cand.shape[1] // spec_count
     local_ids = lax.dynamic_slice_in_dim(cand, position * col_share, col_share, 1)

time: 1350 us -> 1260 us (0.933)
  waiting for transfers between devices: 949 us -> 824 us
  local copies, waits for them, and re-layouts: 267 us -> 283 us
    psum x1 -> x0, waiting for transfers between devices: 227 us -> none  [on_device(): summed = lax.psum(score_tile, 'spec')]
    all_gather x0 -> x1, waiting for transfers between devices: none -> 104 us  [on_device(): summed = jnp.sum(lax.all_gather(score_tile, 'spec'), axis=0)]
    unnamed x15 -> x14, local copies, waits for them, and re-layouts: 2.36 us -> 18 us
where the time goes in v1:
time: 1260 us; the launch traced here: 1250 us
  waiting for transfers between devices  824 us (65%)
  local copies, waits for them, and re-layouts  283 us (22%)
  blocking collectives  78.1 us (6%)
  other arithmetic  31.9 us (3%)
  between operations  15.7 us (1%)
  matrix products  13.8 us (1%)
    psum x8, waiting for transfers between devices, broadcast(): return lax.psum(kept, axis)  720 us
    gather x1, local copies, waits for them, and re-layouts, zscores(): picked = jnp.take_along_axis(score_tile, cand_ids, axis=1)  261 us
    all_gather x1, waiting for transfers between devices, on_device(): summed = jnp.sum(lax.all_gather(score_tile, 'spec'), axis=0)  104 us
    unnamed x1, blocking collectives  78.1 us
  transfers between devices with their start and end apart: 11, of which 10 were waited for; matrix products, arithmetic and copies ran while one was open for 0% of the time, Pallas kernels for 0%

profile of v1, /device:TPU:1, one launch (start us, length us, event | category | flops | bytes accessed | tf_op | source)
XLA Modules:
  0.0 1254.8 jit_solution(283753409662075569)
XLA Ops:
  8.0 1.5 copy.29
  9.5 5.1 collective-permute-start.1
  14.7 1.9 collective-permute-start
  16.6 0.1 broadcast_in_dim.32
  16.7 0.1 le.27
  16.8 0.1 subtract_abs_fusion
  16.9 0.5 broadcast_compare_fusion
  17.4 0.1 broadcast_bitcast_fusion
  17.5 0.3 collective-permute-done
  17.8 1.4 concatenate.3
  19.2 0.3 pad.4
  19.5 0.4 fusion.2
  20.0 0.4 fusion.4
  20.4 1.8 add_add_fusion
  22.2 1.9 copy.35
  24.2 1.6 subtract_convert_fusion
  25.9 737.4 %while.15 = (s32[]{:T(128)}, f32[256,512]{0,1:T(8,128)S(1)}, bf16[64,2048]{1,0:T(8,128)(2,1)S(1)}, bf16[256,2048]{1,0:T(8,128)(2,1)S(1)}, s32[]{:T(128)}, /*index=5*/s32[]{:T(128)}, s32[]{:T(128)}, s32[]{:T(128)}, u32[]{:T(128)}) while((s32[]{:T(128)}, f32[256,512]{0,1:T(8,128)S(1)}, bf16[64,2048]{1,0:T(8,128)(2,1)S(1)}, ...), condition=%wide.region_2.3_spmd, body=%wide.region_0.2_spmd.sunk | while | flops 67371016 | bytes 3473629 | solution.py:81
  25.9 0.0 all-reduce.4.cloned.1.call-start
  25.9 0.7 broadcast_select_fusion.2
  26.7 90.9 %all-reduce.4.cloned.1.call-done = bf16[64,2048]{1,0:T(8,128)(2,1)} async-done(((bf16[64,2048]{1,0:T(8,128)(2,1)}), bf16[64,2048]{1,0:T(8,128)(2,1)}) %all-reduce.4.cloned.1.call-update) | async-done | bytes 262160 | tf_op jit(solution)/shard_map/while/body/eval_jaxpr/psum | solution.py:25
  117.6 1.4 fusion.19
  119.0 0.0 all-reduce.4.cloned.1.call-start
  119.1 0.7 broadcast_select_fusion.2
  119.8 90.0 %all-reduce.4.cloned.1.call-done = bf16[64,2048]{1,0:T(8,128)(2,1)} async-done(((bf16[64,2048]{1,0:T(8,128)(2,1)}), bf16[64,2048]{1,0:T(8,128)(2,1)}) %all-reduce.4.cloned.1.call-update) | async-done | bytes 262160 | tf_op jit(solution)/shard_map/while/body/eval_jaxpr/psum | solution.py:25
  209.8 1.4 fusion.19
  211.2 0.0 all-reduce.4.cloned.1.call-start
  211.3 0.7 broadcast_select_fusion.2
  212.0 89.9 %all-reduce.4.cloned.1.call-done = bf16[64,2048]{1,0:T(8,128)(2,1)} async-done(((bf16[64,2048]{1,0:T(8,128)(2,1)}), bf16[64,2048]{1,0:T(8,128)(2,1)}) %all-reduce.4.cloned.1.call-update) | async-done | bytes 262160 | tf_op jit(solution)/shard_map/while/body/eval_jaxpr/psum | solution.py:25
  302.0 1.4 fusion.19
  303.4 0.0 all-reduce.4.cloned.1.call-start
  303.4 0.7 broadcast_select_fusion.2
  304.2 89.6 %all-reduce.4.cloned.1.call-done = bf16[64,2048]{1,0:T(8,128)(2,1)} async-done(((bf16[64,2048]{1,0:T(8,128)(2,1)}), bf16[64,2048]{1,0:T(8,128)(2,1)}) %all-reduce.4.cloned.1.call-update) | async-done | bytes 262160 | tf_op jit(solution)/shard_map/while/body/eval_jaxpr/psum | solution.py:25
  393.8 1.4 fusion.19
  395.2 0.0 all-reduce.4.cloned.1.call-start
  395.3 0.7 broadcast_select_fusion.2
  396.0 89.6 %all-reduce.4.cloned.1.call-done = bf16[64,2048]{1,0:T(8,128)(2,1)} async-done(((bf16[64,2048]{1,0:T(8,128)(2,1)}), bf16[64,2048]{1,0:T(8,128)(2,1)}) %all-reduce.4.cloned.1.call-update) | async-done | bytes 262160 | tf_op jit(solution)/shard_map/while/body/eval_jaxpr/psum | solution.py:25
  485.7 1.4 fusion.19
  487.1 0.0 all-reduce.4.cloned.1.call-start
  487.1 0.7 broadcast_select_fusion.2
  487.9 89.6 %all-reduce.4.cloned.1.call-done = bf16[64,2048]{1,0:T(8,128)(2,1)} async-done(((bf16[64,2048]{1,0:T(8,128)(2,1)}), bf16[64,2048]{1,0:T(8,128)(2,1)}) %all-reduce.4.cloned.1.call-update) | async-done | bytes 262160 | tf_op jit(solution)/shard_map/while/body/eval_jaxpr/psum | solution.py:25
  577.5 1.4 fusion.19
  578.9 0.0 all-reduce.4.cloned.1.call-start
  579.0 0.7 broadcast_select_fusion.2
  579.7 90.0 %all-reduce.4.cloned.1.call-done = bf16[64,2048]{1,0:T(8,128)(2,1)} async-done(((bf16[64,2048]{1,0:T(8,128)(2,1)}), bf16[64,2048]{1,0:T(8,128)(2,1)}) %all-reduce.4.cloned.1.call-update) | async-done | bytes 262160 | tf_op jit(solution)/shard_map/while/body/eval_jaxpr/psum | solution.py:25
  669.7 1.4 fusion.19
  671.2 0.7 broadcast_select_fusion.2
  671.9 90.0 %all-reduce.4.cloned.1.call-done = bf16[64,2048]{1,0:T(8,128)(2,1)} async-done(((bf16[64,2048]{1,0:T(8,128)(2,1)}), bf16[64,2048]{1,0:T(8,128)(2,1)}) %all-reduce.4.cloned.1.call-update) | async-done | bytes 262160 | tf_op jit(solution)/shard_map/while/body/eval_jaxpr/psum | solution.py:25
  761.9 1.4 fusion.19
  763.3 0.2 all-gather.3.cloned.1.call-start
  763.5 0.5 copy-done.1
  764.1 0.1 constant_dynamic-slice_fusion
  764.2 0.1 reshape.69
  764.4 104.4 %all-gather.3.cloned.1.call-done = f32[8192,512]{0,1:T(8,128)} async-done(((f32[256,512]{0,1:T(8,128)}), f32[8192,512]{0,1:T(8,128)}) %all-gather.3.cloned.1.call-update) | async-done | bytes 16777232 | tf_op jit(solution)/shard_map/all_gather | solution.py:82
  868.8 6.5 reduce.1
  875.4 15.8 %copy.40 = f32[64,8,32,256]{3,2,1,0:T(8,128)} copy(f32[64,8,32,256]{3,1,2,0:T(8,128)} %bitcast.45) | data formatting | bytes 33554432
  891.2 8.7 bitcast_reduce_fusion
  899.9 260.6 %gather_fusion = f32[32768]{0:T(1024)S(1)} fusion(f32[256,512]{0,1:T(8,128)S(1)} %bitcast_reduce_fusion, s32[32768]{0:T(1024)S(1)} %fusion.8), kind=kCustom, calls=%fused_computation | custom fusion | bytes 524288 | tf_op jit(solution)/shard_map/jit(take_along_axis)/gather | solution.py:39
  1160.5 0.1 multiply_reduce_fusion
  1160.6 0.1 fusion.7
  1160.7 0.1 compare_select_fusion
  1160.9 0.1 reshape.71
  1161.0 7.6 scatter_custom_fusion
  1168.6 78.1 %all-reduce.1 = f32[512]{0:T(512)S(1)} all-reduce(f32[512]{0:T(512)S(1)} %scatter_custom_fusion), channel_id=3, replica_groups=mesh['spec'=32,'bucket'=8] {'spec','bucket'}, use_global_device_ids=true, to_apply=%region_7.8.clone | all-reduce | flops 512 | bytes 4096
  1246.8 0.6 dynamic-slice_multiply_fusion
  (30 shorter events, 0.4 us)
Async XLA Ops:
  8.0 8.6 copy-start.4
  9.5 8.0 collective-permute-start.1
  14.7 3.1 collective-permute-start
  24.2 1.7 copy-start
  25.8 738.3 %copy-start.2 = (s32[256,128]{1,0:T(8,128)S(1)}, s32[256,128]{1,0:T(8,128)}, u32[]{:S(2)}) copy-start(s32[256,128]{1,0:T(8,128)} %param.8) | copy-start | bytes 393220
  25.9 91.8 %all-reduce.4.cloned.1.call-start = ((), (), s32[]{:S(2)}) async-start(), calls=%async_computation.1 | async-start | bytes 524288 | tf_op jit(solution)/shard_map/while/body/eval_jaxpr/psum | solution.py:25
  119.0 90.8 %all-reduce.4.cloned.1.call-start = ((), (), s32[]{:S(2)}) async-start(), calls=%async_computation.1 | async-start | bytes 524288 | tf_op jit(solution)/shard_map/while/body/eval_jaxpr/psum | solution.py:25
  211.2 90.8 %all-reduce.4.cloned.1.call-start = ((), (), s32[]{:S(2)}) async-start(), calls=%async_computation.1 | async-start | bytes 524288 | tf_op jit(solution)/shard_map/while/body/eval_jaxpr/psum | solution.py:25
  303.4 90.5 %all-reduce.4.cloned.1.call-start = ((), (), s32[]{:S(2)}) async-start(), calls=%async_computation.1 | async-start | bytes 524288 | tf_op jit(solution)/shard_map/while/body/eval_jaxpr/psum | solution.py:25
  395.2 90.5 %all-reduce.4.cloned.1.call-start = ((), (), s32[]{:S(2)}) async-start(), calls=%async_computation.1 | async-start | bytes 524288 | tf_op jit(solution)/shard_map/while/body/eval_jaxpr/psum | solution.py:25
  487.1 90.5 %all-reduce.4.cloned.1.call-start = ((), (), s32[]{:S(2)}) async-start(), calls=%async_computation.1 | async-start | bytes 524288 | tf_op jit(solution)/shard_map/while/body/eval_jaxpr/psum | solution.py:25
  578.9 90.8 %all-reduce.4.cloned.1.call-start = ((), (), s32[]{:S(2)}) async-start(), calls=%async_computation.1 | async-start | bytes 524288 | tf_op jit(solution)/shard_map/while/body/eval_jaxpr/psum | solution.py:25
  671.1 90.8 %all-reduce.4.cloned.1.call-start = ((), (), s32[]{:S(2)}) async-start(), calls=%async_computation.1 | async-start | bytes 524288 | tf_op jit(solution)/shard_map/while/body/eval_jaxpr/psum | solution.py:25
  763.3 0.8 copy-start.1
  763.3 105.5 %all-gather.3.cloned.1.call-start = ((), (), s32[]{:S(2)}) async-start(), calls=%async_computation | async-start | bytes 17301504 | tf_op jit(solution)/shard_map/all_gather | solution.py:82
  1160.7 86.6 %copy-start.3 = (f32[256,128]{1,0:T(8,128)}, f32[256,128]{1,0:T(8,128)S(1)}, u32[]{:S(2)}) copy-start(f32[256,128]{1,0:T(8,128)S(1)} %fusion.7) | copy-start | bytes 393220
Sparse Core Ops, SparseCore 0:
  29.3 88.2 all-reduce.3
  122.5 87.2 all-reduce.3
  214.6 87.2 all-reduce.3
  306.5 87.2 all-reduce.3
  398.4 87.2 all-reduce.3
  490.2 87.2 all-reduce.3
  582.4 87.2 all-reduce.3
  674.6 87.2 all-reduce.3
Sparse Core Ops, SparseCore 1:
  765.6 103.1 all-gather.2
